TPU v7x, 32 devices: a whole 2x2x4 slice. The times are simulated.
32 devices in a mesh: blk: 8 (over y, x, core), orb: 4 (over z).
Axes of the slice: x: 2, y: 2, z: 4, core: 2. Of those that a mesh axis runs over, the one named last changes fastest.
Arguments:
- green_tiles: bfloat16 [2, 192, 256, 256], P(None, 'blk'), may hold values from -6 to 6
- screen_tiles: bfloat16 [2, 96, 256, 256], P(None, 'blk', 'orb'), may hold values from -6 to 6
- coeffs: bfloat16 [12288, 2048], P('blk', 'orb'), may hold values from -0.099609375 to 0.099609375
- tile_count: int32 [8], P('blk'), may hold values from 1 to 24, 96 in all
- send_slot: int32 [8, 8, 3], P('blk'), may hold values from 0 to 11
- recv_index: int32 [8, 24], P('blk'), may hold values from 0 to 23, as said below
- row_block: int32 [8, 24], P('blk'), may hold values from 0 to 5
- col_block: int32 [8, 24], P('blk'), may hold values from 0 to 47
Outputs:
- sigma_orbital: float32 [2048, 2, 2048], P('blk', None, 'orb')
Inputs may be any that keep to these rules, and one draw needn't show every extreme that they name: `recv_index`: for each blk index and each round r < 3, the slots r * (8) to (r + 1) * 8 - 1 name every peer once, each as peer * 3 + r. `tile_count`: the counts of all blk indices sum to 96.
All inputs are finite; a program needn't handle non-finite values. No bound on the sum of `tile_count` on one device may be relied on, other than what follows from the above.
Results may differ from a plain program's by a relative error of at most 0.0041.
Values may be sent and summed in bfloat16 or wider, within the bound.
A program may use at most 128 MiB of HBM per device.

v0:
```python
import jax
import jax.numpy as jnp
from jax import lax
from jax.sharding import PartitionSpec as P


def shards(
    green_tiles, screen_tiles, coeffs, tile_count, send_slot, recv_index, row_block, col_block
):
    width = green_tiles.shape[2]
    slot_total = green_tiles.shape[1]
    owned_blocks = coeffs.shape[0] // width
    orbital_local = coeffs.shape[1]
    outgoing = send_slot.reshape(-1)
    screen_whole = lax.all_gather(screen_tiles, "orb", axis=2, tiled=True)
    packed = jnp.take(screen_whole, outgoing, axis=1)
    arrived = lax.all_to_all(packed, "blk", split_axis=1, concat_axis=1, tiled=True)
    panel = lax.all_gather(coeffs, "blk", axis=0, tiled=True)
    panel_blocks = panel.reshape(-1, width, orbital_local)
    own_rows = lax.all_gather(coeffs, "orb", axis=1, tiled=True)
    live = (jnp.arange(slot_total, dtype=jnp.int32) < tile_count[0]).astype(jnp.float32)
    targets = row_block[0]
    group = 8

    def accumulate(totals, start):
        green_part = lax.dynamic_slice_in_dim(green_tiles, start, group, 1)
        which = lax.dynamic_slice_in_dim(recv_index[0], start, group, 0)
        screen_part = jnp.take(arrived, which, axis=1)
        sigma = (-(green_part.astype(jnp.float32) * screen_part.astype(jnp.float32))).astype(
            jnp.bfloat16
        )
        columns = lax.dynamic_slice_in_dim(col_block[0], start, group, 0)
        blocks = jnp.take(panel_blocks, columns, axis=0)
        products = jnp.einsum("tsab,sbm->satm", sigma, blocks, preferred_element_type=jnp.float32)
        group_rows = lax.dynamic_slice_in_dim(targets, start, group, 0)
        group_live = lax.dynamic_slice_in_dim(live, start, group, 0)
        for member in range(group):
            target = group_rows[member]
            current = lax.dynamic_index_in_dim(totals, target, 0, keepdims=True)
            updated = current + group_live[member] * products[member][None]
            totals = lax.dynamic_update_slice_in_dim(totals, updated, target, 0)
        return (totals, None)

    starts = jnp.arange(0, slot_total, group, dtype=jnp.int32)
    empty = jnp.zeros((owned_blocks, width, 2, orbital_local), jnp.float32)
    totals, unused = lax.scan(accumulate, empty, starts)
    folded = totals.astype(jnp.bfloat16).reshape(owned_blocks * width, 2, orbital_local)
    return lax.psum_scatter(
        jnp.einsum("kn,ktm->ntm", own_rows, folded, preferred_element_type=jnp.float32),
        "blk",
        scatter_dimension=0,
        tiled=True,
    )


def solution(mesh):
    return jax.shard_map(
        shards,
        mesh=mesh,
        in_specs=(
            P(None, "blk", None, None),
            P(None, "blk", "orb", None),
            P("blk", "orb"),
            P("blk"),
            P("blk", None, None),
            P("blk", None),
            P("blk", None),
            P("blk", None),
        ),
        out_specs=P("blk", None, "orb"),
        check_vma=False,
    )
```

profile of v0, /device:TPU:0, one launch (start us, length us, event | category | flops | bytes accessed | tf_op | source)
XLA Modules:
  0.0 496.8 jit_solution(7030310610212735367)
XLA Ops:
  9.0 66.2 %all-gather.6.cloned.1.call-done = bf16[2,12,256,256]{3,2,1,0:T(8,128)(2,1)} async-done(((bf16[2,12,64,256]{3,2,1,0:T(8,128)(2,1)}), bf16[2,12,256,256]{3,2,1,0:T(8,128)(2,1)}) %all-gather.6.cloned.1.call-update) | async-done | bytes 3145744 | tf_op jit(solution)/shard_map/all_gather | solution.py:15
  75.1 6.3 %gather_fusion.2 = bf16[24,2,256,256]{3,2,1,0:T(8,128)(2,1)} fusion(bf16[2,12,256,256]{3,2,1,0:T(8,128)(2,1)} %all-gather.6.cloned.1.call-done, s32[1024]{0:T(1024)S(1)} %pad_clamp_fusion.2), kind=kCustom, calls=%fused_computation.2 | custom fusion | bytes 12583008 | tf_op jit(solution)/shard_map/jit(_take)/gather | solution.py:16
  81.4 7.0 %select_bitcast_fusion = bf16[2,24,256,256]{3,2,0,1:T(8,128)(2,1)} fusion(bf16[24,2,256,256]{3,2,1,0:T(8,128)(2,1)} %gather_fusion.2, pred[24]{0:T(512)(128)(4,1)S(1)} %compare_and_fusion.2), kind=kLoop, calls=%fused_computation.55 | loop fusion | flops 3145728 | bytes 12582936 | tf_op jit(solution)/shard_map/jit(_take)/select_n | solution.py:16
  88.4 4.8 all-to-all-start
  94.6 108.7 %all-to-all-done = bf16[2,24,256,256]{3,2,0,1:T(8,128)(2,1)} async-done(((bf16[2,24,256,256]{3,2,0,1:T(8,128)(2,1)}), bf16[2,24,256,256]{3,2,0,1:T(8,128)(2,1)}, u32[]{:S(2)}, u32[]{:S(2)}) %all-to-all-start) | async-done | bytes 6291488 | tf_op jit(solution)/shard_map/all_to_all | solution.py:17
  203.4 6.1 %copy.18 = bf16[2,24,256,256]{3,2,1,0:T(8,128)(2,1)} copy(bf16[2,24,256,256]{3,2,0,1:T(8,128)(2,1)} %all-to-all-done) | data formatting | bytes 12582912 | tf_op jit(solution)/shard_map/while | solution.py:46
  212.7 189.8 %while.10 = (s32[]{:T(128)}, f32[6,256,2,512]{1,3,2,0:T(8,128)}, s32[3]{0:T(128)S(1)}, s32[24]{0:T(128)S(1)}, f32[24]{0:T(128)S(1)}, /*index=5*/s32[1,24]{1,0:T(...) while((s32[]{:T(128)}, f32[6,256,2,512]{1,3,2,0:T(8,128)}, ...), condition=%wide.region_1.2_spmd, body=%wide.region_0.1_spmd.sunk | while | flops 1085278336 | bytes 48247880 | solution.py:46
  215.6 4.2 gather_fusion
  219.8 6.9 %gather_fusion.1 = bf16[8,256,512]{2,1,0:T(8,128)(2,1)} fusion(bf16[48,256,512]{2,1,0:T(8,128)(2,1)} %get-tuple-element.253, s32[1024]{0:T(1024)S(1)} %pad_clamp_fusion.6), kind=kCustom, calls=%fused_computation.clone.1 | custom fusion | bytes 4194336 | tf_op jit(solution)/shard_map/while/body/eval_jaxpr/jit(_take)/gather | solution.py:33
  226.8 7.5 %convolution_bitcast_fusion.2 = f32[8,256,2,512]{1,3,2,0:T(8,128)} fusion(bf16[8,2,256,256]{3,2,1,0:T(8,128)(2,1)S(1)} %gather_fusion, bf16[8,256,512]{2,1,0:T(8,128)(2,1)} %gather_fusion.1, pred[8]{0:T(512)(128)(4,1)S(1)} %get-tuple-element.202, pred[8]{0:T(512)(128)(4,1)S(1)} %get-tuple-element.203, ...), kind=kOutput, calls=%fused_computation.6.clone.1 | convolution fusion | flops 1081081856 | bytes 14680084 | tf_op jit(solution)/shard_map/while/body/eval_jaxpr/tsab,sbm->satm/dot_general | solution.py:34
  252.7 3.3 fusion.60
  257.9 3.3 fusion.61
  268.1 3.4 fusion.63
  273.3 3.3 fusion.64
  279.5 3.5 gather_fusion
  282.9 6.7 %gather_fusion.1 = bf16[8,256,512]{2,1,0:T(8,128)(2,1)} fusion(bf16[48,256,512]{2,1,0:T(8,128)(2,1)} %get-tuple-element.253, s32[1024]{0:T(1024)S(1)} %pad_clamp_fusion.6), kind=kCustom, calls=%fused_computation.clone.1 | custom fusion | bytes 4194336 | tf_op jit(solution)/shard_map/while/body/eval_jaxpr/jit(_take)/gather | solution.py:33
  289.7 7.4 %convolution_bitcast_fusion.2 = f32[8,256,2,512]{1,3,2,0:T(8,128)} fusion(bf16[8,2,256,256]{3,2,1,0:T(8,128)(2,1)S(1)} %gather_fusion, bf16[8,256,512]{2,1,0:T(8,128)(2,1)} %gather_fusion.1, pred[8]{0:T(512)(128)(4,1)S(1)} %get-tuple-element.202, pred[8]{0:T(512)(128)(4,1)S(1)} %get-tuple-element.203, ...), kind=kOutput, calls=%fused_computation.6.clone.1 | convolution fusion | flops 1081081856 | bytes 14680084 | tf_op jit(solution)/shard_map/while/body/eval_jaxpr/tsab,sbm->satm/dot_general | solution.py:34
  310.6 3.3 fusion.59
  315.8 3.3 fusion.60
  326.2 3.3 fusion.62
  331.2 3.3 fusion.63
  336.4 3.3 fusion.64
  342.5 3.5 gather_fusion
  346.0 6.6 %gather_fusion.1 = bf16[8,256,512]{2,1,0:T(8,128)(2,1)} fusion(bf16[48,256,512]{2,1,0:T(8,128)(2,1)} %get-tuple-element.253, s32[1024]{0:T(1024)S(1)} %pad_clamp_fusion.6), kind=kCustom, calls=%fused_computation.clone.1 | custom fusion | bytes 4194336 | tf_op jit(solution)/shard_map/while/body/eval_jaxpr/jit(_take)/gather | solution.py:33
  352.7 7.4 %convolution_bitcast_fusion.2 = f32[8,256,2,512]{1,3,2,0:T(8,128)} fusion(bf16[8,2,256,256]{3,2,1,0:T(8,128)(2,1)S(1)} %gather_fusion, bf16[8,256,512]{2,1,0:T(8,128)(2,1)} %gather_fusion.1, pred[8]{0:T(512)(128)(4,1)S(1)} %get-tuple-element.202, pred[8]{0:T(512)(128)(4,1)S(1)} %get-tuple-element.203, ...), kind=kOutput, calls=%fused_computation.6.clone.1 | convolution fusion | flops 1081081856 | bytes 14680084 | tf_op jit(solution)/shard_map/while/body/eval_jaxpr/tsab,sbm->satm/dot_general | solution.py:34
  373.5 3.3 fusion.59
  383.9 3.3 fusion.61
  394.0 3.3 fusion.63
  399.2 3.3 fusion.64
  402.5 4.0 copy.19
  406.5 10.8 %fusion.32 = f32[2048,2,512]{0,2,1:T(8,128)} fusion(bf16[1536,2,512]{2,0,1:T(8,128)(2,1)S(1)} %bitcast.107, bf16[1536,2048]{1,0:T(8,128)(2,1)} %all-gather.8.cloned.1.call-done), kind=kOutput, calls=%fused_computation.56 | convolution fusion | flops 6442450944 | bytes 17825792 | tf_op jit(solution)/shard_map/kn,ktm->ntm/dot_general | solution.py:49
  417.4 70.7 %reduce-scatter.2.cloned.1.call-done = f32[256,2,512]{0,2,1:T(8,128)} async-done(((f32[2048,2,512]{0,2,1:T(8,128)}), f32[256,2,512]{0,2,1:T(8,128)}) %reduce-scatter.2.cloned.1.call-update) | async-done | bytes 1048592 | tf_op jit(solution)/shard_map/reduce_scatter | solution.py:48
  (64 shorter events, 51.5 us)
Async XLA Ops:
  6.5 68.6 %all-gather.6.cloned.1.call-start = ((), (), s32[]{:S(2)}) async-start(), calls=%async_computation.3 | async-start | bytes 3932160 | tf_op jit(solution)/shard_map/all_gather | solution.py:15
  7.3 202.2 %all-gather.4.cloned.1.call-start = ((), (), s32[]{:S(2)}) async-start(), calls=%async_computation.2 | async-start | bytes 14155776 | tf_op jit(solution)/shard_map/all_gather | solution.py:18
  88.4 115.0 %all-to-all-start = ((bf16[2,24,256,256]{3,2,0,1:T(8,128)(2,1)}), bf16[2,24,256,256]{3,2,0,1:T(8,128)(2,1)}, u32[]{:S(2)}, u32[]{:S(2)}) async-start(bf16[2,24,256,256]{3,2,0,1:T(8,128)(2,1)} %select_bitcast_fusion), calls=%async_computation | async-start | bytes 12582912 | tf_op jit(solution)/shard_map/all_to_all | solution.py:17
  93.2 313.3 %all-gather.8.cloned.1.call-start = ((), (), s32[]{:S(2)}) async-start(), calls=%async_computation.4 | async-start | bytes 7864320 | tf_op jit(solution)/shard_map/all_gather | solution.py:20
  93.9 394.1 %reduce-scatter.2.cloned.1.call-start = ((), (), s32[]{:S(2)}) async-start(), calls=%async_computation.5 | async-start | bytes 9437184 | tf_op jit(solution)/shard_map/reduce_scatter | solution.py:48
  209.5 3.3 copy-start
  209.5 3.3 copy-start.1
  209.5 3.3 copy-start.2
Sparse Core Ops, SparseCore 0:
  8.9 66.1 all-gather.5
  77.0 130.5 all-gather.3
  209.2 115.3 all-gather.7
  417.5 70.4 reduce-scatter.1
where the time goes:
time: 499 us; the launch traced here: 497 us
  waiting for transfers between devices  248 us (50%)
  other arithmetic  86.4 us (17%)
  local copies, waits for them, and re-layouts  60.6 us (12%)
  loops' own time  50.2 us (10%)
  matrix products  33.2 us (7%)
  between operations  13.8 us (3%)
    all_to_all x1, waiting for transfers between devices, shards(): lax.all_to_all(packed, 'blk', split_axis=1, concat_axis=1, tiled=True)  109 us
    dynamic_update_slice x24, other arithmetic, accumulate(): totals = lax.dynamic_update_slice_in_dim(totals, updated, target, 0)  78.9 us
    reduce_scatter x1, waiting for transfers between devices, shards(): lax.psum_scatter(jnp.einsum('kn,ktm->ntm', own_rows, folded, preferred_el...  70.7 us
    all_gather x1, waiting for transfers between devices, shards(): screen_whole = lax.all_gather(screen_tiles, 'orb', axis=2, tiled=True)  66.2 us
    another operation x1, loops' own time, shards(): totals, unused = lax.scan(accumulate, empty, starts)  50.2 us
    dot_general x3, matrix products, accumulate(): jnp.einsum('tsab,sbm->satm', sigma, blocks, preferred_element_type=jnp.fl...  22.3 us
    gather x3, local copies, waits for them, and re-layouts, accumulate(): blocks = jnp.take(panel_blocks, columns, axis=0)  20.2 us
    gather x3, local copies, waits for them, and re-layouts, accumulate(): screen_part = jnp.take(arrived, which, axis=1)  11.1 us
  transfers between devices with their start and end apart: 5, of which 3 were waited for; matrix products, arithmetic and copies ran while one was open for 34% of the time, Pallas kernels for 0%

commit v1 on v0

v1 whole, which is shorter than its diff:
```python
import functools

import jax
import jax.numpy as jnp
from jax import lax
from jax.experimental import pallas as pl
from jax.experimental.pallas import tpu as pltpu
from jax.sharding import PartitionSpec as P

MESH = pl.DeviceIdType.MESH
ANY = pl.BlockSpec(memory_space=pl.ANY)


def flip(index, mask):
    bit = 1
    while bit <= mask:
        if mask & bit:
            index = index + bit * (1 - 2 * lax.rem(lax.div(index, bit), 2))
        bit *= 2
    return index


def remote(src, dst, send, recv, blk, orb):
    return pltpu.make_async_remote_copy(
        src_ref=src, dst_ref=dst, send_sem=send, recv_sem=recv,
        device_id=(blk, orb), device_id_type=MESH,
    )


def greet(barrier, blk, orb):
    pl.semaphore_signal(barrier, inc=1, device_id=(blk, orb), device_id_type=MESH)


def gather_kernel(n_blk, n_orb, screen, coeffs, whole, panel, local, zsend, zrecv,
                  psend, precv, fsend, frecv):
    me, z = lax.axis_index("blk"), lax.axis_index("orb")
    partner = flip(me, 1)
    masks = list(range(2, n_blk, 2))
    barrier = pltpu.get_barrier_semaphore()

    @pl.when(z > 0)
    def _():
        greet(barrier, me, z - 1)

    @pl.when(z < n_orb - 1)
    def _():
        greet(barrier, me, z + 1)

    for mask in [1] + masks:
        greet(barrier, flip(me, mask), z)
    pl.semaphore_wait(barrier, len(masks) + 1 + jnp.minimum(z, 1) + jnp.minimum(n_orb - 1 - z, 1))

    def down(src, block):
        return remote(block, whole.at[src], zsend.at[0, src], zrecv.at[src], me, z - 1)

    def up(src, block):
        return remote(block, whole.at[src], zsend.at[1, src], zrecv.at[src], me, z + 1)

    @pl.when(z > 0)
    def _():
        down(z, screen).start()

    @pl.when(z < n_orb - 1)
    def _():
        up(z, screen).start()

    def direct(mask):
        return remote(coeffs, panel.at[me], psend.at[mask // 2], precv.at[mask // 2], flip(me, mask), z)

    for mask in masks:
        direct(mask).start()

    def forward(mask):
        owner = flip(me, mask)
        block = coeffs if mask == 0 else panel.at[owner]
        return remote(block, panel.at[owner], fsend.at[mask // 2], frecv.at[mask // 2], partner, z)

    forward(0).start()
    own_screen = pltpu.make_async_copy(screen, whole.at[z], local.at[0])
    own_coeffs = pltpu.make_async_copy(coeffs, panel.at[me], local.at[1])
    own_screen.start()
    own_coeffs.start()

    for step in range(1, max(n_orb, len(masks) + 1)):
        if step < n_orb:
            @pl.when(z - step >= 0)
            def _():
                src = z - step
                up(src, whole.at[src]).wait_recv()

                @pl.when(z < n_orb - 1)
                def _():
                    up(src, whole.at[src]).start()

            @pl.when(z + step < n_orb)
            def _():
                src = z + step
                down(src, whole.at[src]).wait_recv()

                @pl.when(z > 0)
                def _():
                    down(src, whole.at[src]).start()
        if step - 1 < len(masks):
            mask = masks[step - 1]
            owner = flip(me, mask)
            remote(coeffs, panel.at[owner], psend.at[mask // 2], precv.at[mask // 2], owner, z).wait_recv()
            forward(mask).start()

    own_screen.wait()
    own_coeffs.wait()
    for mask in masks:
        direct(mask).wait_send()
    for mask in [0] + masks:
        forward(mask).wait_send()
        owner = flip(partner, mask)
        remote(coeffs, panel.at[owner], fsend.at[mask // 2], frecv.at[mask // 2], partner, z).wait_recv()

    for src in range(n_orb):
        @pl.when((z > 0) & (src >= z))
        def _():
            down(src, whole.at[src]).wait_send()

        @pl.when((z < n_orb - 1) & (src <= z))
        def _():
            up(src, whole.at[src]).wait_send()


def gather(screen, coeffs, n_blk, n_orb):
    dma = pltpu.SemaphoreType.DMA
    return pl.pallas_call(
        functools.partial(gather_kernel, n_blk, n_orb),
        out_shape=(
            jax.ShapeDtypeStruct((n_orb,) + screen.shape, screen.dtype),
            jax.ShapeDtypeStruct((n_blk,) + coeffs.shape, coeffs.dtype),
        ),
        in_specs=[ANY, ANY],
        out_specs=(ANY, ANY),
        scratch_shapes=[
            dma((2,)), dma((2, n_orb)), dma((n_orb,)),
            dma((n_blk // 2,)), dma((n_blk // 2,)), dma((n_blk // 2,)), dma((n_blk // 2,)),
        ],
        compiler_params=pltpu.CompilerParams(collective_id=1, has_side_effects=True),
        name="gather",
    )(screen, coeffs)


def pack(whole, outgoing):
    n_orb, times, _, rows, width = whole.shape
    total = outgoing.shape[0]

    def body(slots, tile, out):
        for q in range(n_orb):
            out[0, :, q * rows:(q + 1) * rows, :] = tile[q, :, 0]

    return pl.pallas_call(
        body,
        out_shape=jax.ShapeDtypeStruct((total, times, n_orb * rows, width), whole.dtype),
        grid_spec=pltpu.PrefetchScalarGridSpec(
            num_scalar_prefetch=1,
            grid=(total,),
            in_specs=[pl.BlockSpec((n_orb, times, 1, rows, width), lambda j, slots: (0, 0, slots[j], 0, 0))],
            out_specs=pl.BlockSpec((1, times, n_orb * rows, width), lambda j, slots: (j, 0, 0, 0)),
        ),
        name="pack",
    )(outgoing, whole)


def exchange_kernel(n_blk, packed, arrived, local, send, recv):
    me, z = lax.axis_index("blk"), lax.axis_index("orb")
    barrier = pltpu.get_barrier_semaphore()
    for mask in range(1, n_blk):
        greet(barrier, flip(me, mask), z)
    pl.semaphore_wait(barrier, n_blk - 1)

    def copy(mask):
        peer = flip(me, mask)
        return remote(packed.at[peer], arrived.at[me], send.at[mask], recv.at[mask], peer, z)

    order = sorted(range(1, n_blk), key=lambda mask: -bin(mask).count("1"))
    for mask in order:
        copy(mask).start()
    own = pltpu.make_async_copy(packed.at[me], arrived.at[me], local)
    own.start()
    own.wait()
    for mask in order:
        copy(mask).wait_send()
        peer = flip(me, mask)
        remote(packed.at[peer], arrived.at[peer], send.at[mask], recv.at[mask], peer, z).wait_recv()


def exchange(packed, n_blk):
    dma = pltpu.SemaphoreType.DMA
    return pl.pallas_call(
        functools.partial(exchange_kernel, n_blk),
        out_shape=jax.ShapeDtypeStruct(packed.shape, packed.dtype),
        in_specs=[ANY],
        out_specs=ANY,
        scratch_shapes=[dma, dma((n_blk,)), dma((n_blk,))],
        compiler_params=pltpu.CompilerParams(collective_id=2, has_side_effects=True),
        name="exchange",
    )(packed)


def rows_kernel(count, codes, targets, columns, green, screen, block, out, acc):
    slot = pl.program_id(0)
    orbitals = block.shape[2]

    @pl.when(slot == 0)
    def _():
        acc[...] = jnp.zeros_like(acc)

    @pl.when(slot < count[0])
    def _():
        target = targets[slot]
        for t in range(green.shape[0]):
            sigma = (-(green[t, 0].astype(jnp.float32) * screen[0, t].astype(jnp.float32))).astype(jnp.bfloat16)
            acc[target, :, t * orbitals:(t + 1) * orbitals] += jnp.dot(
                sigma, block[0], preferred_element_type=jnp.float32
            )

    @pl.when(slot == pl.num_programs(0) - 1)
    def _():
        for i in range(acc.shape[0]):
            out[i] = acc[i].astype(out.dtype)


def row_sums(green, arrived, blocks, count, codes, targets, columns, owned):
    times, slots, width, _ = green.shape
    orbitals = blocks.shape[2]

    def live(s, count):
        return jnp.minimum(s, count[0] - 1)

    return pl.pallas_call(
        rows_kernel,
        out_shape=jax.ShapeDtypeStruct((owned, width, times * orbitals), jnp.bfloat16),
        grid_spec=pltpu.PrefetchScalarGridSpec(
            num_scalar_prefetch=4,
            grid=(slots,),
            in_specs=[
                pl.BlockSpec((times, 1, width, width), lambda s, n, c, r, k: (0, live(s, n), 0, 0)),
                pl.BlockSpec((1, times, width, width), lambda s, n, c, r, k: (c[live(s, n)], 0, 0, 0)),
                pl.BlockSpec((1, width, orbitals), lambda s, n, c, r, k: (k[live(s, n)], 0, 0)),
            ],
            out_specs=pl.BlockSpec((owned, width, times * orbitals), lambda s, n, c, r, k: (0, 0, 0)),
            scratch_shapes=[pltpu.VMEM((owned, width, times * orbitals), jnp.float32)],
        ),
        compiler_params=pltpu.CompilerParams(vmem_limit_bytes=56 * 2**20),
        name="row_sums",
    )(count, codes, targets, columns, green, arrived, blocks)


def scatter_kernel(n_blk, part, out, first, second, stage, total, ssend, srecv, send, recv):
    me, z = lax.axis_index("blk"), lax.axis_index("orb")
    partner = flip(me, 1)
    masks = sorted(range(2, n_blk, 2), key=lambda mask: -bin(mask).count("1"))
    barrier = pltpu.get_barrier_semaphore()
    for mask in [1] + masks:
        greet(barrier, flip(me, mask), z)
    pl.semaphore_wait(barrier, len(masks) + 1)

    def to_partner(mask):
        h = mask // 2
        return remote(part.at[flip(partner, mask)], first.at[h], ssend.at[h], srecv.at[h], partner, z)

    def to_owner(mask):
        h = mask // 2
        return remote(stage.at[h], second.at[h], send.at[h], recv.at[h], flip(me, mask), z)

    for mask in masks + [0]:
        to_partner(mask).start()
    for mask in masks:
        h = mask // 2
        to_partner(mask).wait_recv()
        stage[h] = (part[flip(me, mask)].astype(jnp.float32) + first[h].astype(jnp.float32)).astype(stage.dtype)
        to_owner(mask).start()
    to_partner(0).wait_recv()
    total[...] = part[me].astype(jnp.float32) + first[0].astype(jnp.float32)
    for mask in masks[::-1]:
        to_owner(mask).wait_recv()
        total[...] += second[mask // 2].astype(jnp.float32)
    out[...] = total[...]
    for mask in masks + [0]:
        to_partner(mask).wait_send()
    for mask in masks:
        to_owner(mask).wait_send()


def scatter(part):
    n_blk, rows, columns = part.shape
    half = n_blk // 2
    dma = pltpu.SemaphoreType.DMA
    vmem = pl.BlockSpec(memory_space=pltpu.VMEM)
    return pl.pallas_call(
        functools.partial(scatter_kernel, n_blk),
        out_shape=jax.ShapeDtypeStruct((rows, columns), jnp.float32),
        in_specs=[vmem],
        out_specs=vmem,
        scratch_shapes=[
            pltpu.VMEM((half, rows, columns), jnp.bfloat16),
            pltpu.VMEM((half, rows, columns), jnp.bfloat16),
            pltpu.VMEM((half, rows, columns), jnp.bfloat16),
            pltpu.VMEM((rows, columns), jnp.float32),
            dma((half,)), dma((half,)), dma((half,)), dma((half,)),
        ],
        compiler_params=pltpu.CompilerParams(
            collective_id=3, has_side_effects=True, vmem_limit_bytes=32 * 2**20
        ),
        name="scatter",
    )(part)


def shards(
    n_blk, n_orb, green_tiles, screen_tiles, coeffs, tile_count, send_slot, recv_index, row_block, col_block
):
    times, _, width, _ = green_tiles.shape
    owned = coeffs.shape[0] // width
    orbitals = coeffs.shape[1]
    whole, panel = gather(screen_tiles, coeffs, n_blk, n_orb)
    own_rows = lax.all_gather(coeffs, "orb", axis=0)
    packed = pack(whole, send_slot.reshape(-1))
    arrived = exchange(packed.reshape((n_blk, -1) + packed.shape[1:]), n_blk)
    folded = row_sums(
        green_tiles, arrived.reshape(packed.shape), panel.reshape(-1, width, orbitals),
        tile_count, recv_index[0], row_block[0], col_block[0], owned,
    ).reshape(owned * width, times * orbitals)
    part = jnp.einsum("zkn,km->znm", own_rows, folded, preferred_element_type=jnp.float32)
    part = part.astype(jnp.bfloat16).reshape(n_blk, -1, times * orbitals)
    return scatter(part).reshape(-1, times, orbitals)


def solution(mesh):
    return jax.shard_map(
        functools.partial(shards, mesh.shape["blk"], mesh.shape["orb"]),
        mesh=mesh,
        in_specs=(
            P(None, "blk", None, None),
            P(None, "blk", "orb", None),
            P("blk", "orb"),
            P("blk"),
            P("blk", None, None),
            P("blk", None),
            P("blk", None),
            P("blk", None),
        ),
        out_specs=P("blk", None, "orb"),
        check_vma=False,
    )
```

time: 499 us -> 325 us (0.65)
  Pallas kernels: 0 us -> 296 us
  waiting for transfers between devices: 248 us -> 0.71 us
  other arithmetic: 86.4 us -> 0 us
  local copies, waits for them, and re-layouts: 60.6 us -> 3.21 us
  loops' own time: 50.2 us -> 0 us
  matrix products: 33.2 us -> 9.81 us
    pallas_call x0 -> x5, Pallas kernels: none -> 296 us  [the longest x1 162 us: gather(): pl.pallas_call(functools.partial(gather_kernel, n_blk, n_orb), out_shape=...]
    all_to_all x1 -> x0, waiting for transfers between devices: 109 us -> none  [shards(): lax.all_to_all(packed, 'blk', split_axis=1, concat_axis=1, tiled=True)]
    dynamic_update_slice x24 -> x0, other arithmetic: 78.9 us -> none  [accumulate(): totals = lax.dynamic_update_slice_in_dim(totals, updated, target, 0)]
    reduce_scatter x1 -> x0, waiting for transfers between devices: 70.7 us -> none  [shards(): lax.psum_scatter(jnp.einsum('kn,ktm->ntm', own_rows, folded, preferred_el...]
    all_gather x3 -> x1, waiting for transfers between devices: 66.2 us -> 0.01 us  [shards(): own_rows = lax.all_gather(coeffs, 'orb', axis=0)]
    another operation x1 -> x0, loops' own time: 50.2 us -> none  [shards(): totals, unused = lax.scan(accumulate, empty, starts)]
    gather x7 -> x0, local copies, waits for them, and re-layouts: 37.6 us -> none  [the longest x3 20.2 us: accumulate(): blocks = jnp.take(panel_blocks, columns, axis=0)]
    dot_general x4 -> x1, matrix products: 33.2 us -> 9.81 us  [shards(): jnp.einsum('zkn,km->znm', own_rows, folded, preferred_element_type=jnp.fl...]
  transfers between devices with their start and end apart: 5 -> 1, of which waited for: 3 -> 0; matrix products, arithmetic and copies ran while one was open for 34% -> 0% of each run, Pallas kernels for 0% -> 83%
where the time goes in v1:
time: 325 us; the launch traced here: 324 us
  Pallas kernels  296 us (91%)
  between operations  14.1 us (4%)
  matrix products  9.81 us (3%)
    pallas_call x1, Pallas kernels, gather(): pl.pallas_call(functools.partial(gather_kernel, n_blk, n_orb), out_shape=...  162 us
    pallas_call x1, Pallas kernels, exchange(): pl.pallas_call(functools.partial(exchange_kernel, n_blk), out_shape=jax.S...  71.1 us
    pallas_call x1, Pallas kernels, scatter(): pl.pallas_call(functools.partial(scatter_kernel, n_blk), out_shape=jax.Sh...  26.2 us
    pallas_call x1, Pallas kernels, row_sums(): pl.pallas_call(rows_kernel, out_shape=jax.ShapeDtypeStruct((owned, width,...  21.6 us
    pallas_call x1, Pallas kernels, pack(): pl.pallas_call(body, out_shape=jax.ShapeDtypeStruct((total, times, n_orb...  15.4 us
    dot_general x1, matrix products, shards(): jnp.einsum('zkn,km->znm', own_rows, folded, preferred_element_type=jnp.fl...  9.81 us
  transfers between devices with their start and end apart: 1, of which 0 were waited for; matrix products, arithmetic and copies ran while one was open for 0% of the time, Pallas kernels for 83%

profile of v1, /device:TPU:0, one launch (start us, length us, event | category | flops | bytes accessed | tf_op | source)
XLA Modules:
  0.0 323.7 jit_solution(2715113112257978688)
XLA Ops:
  6.5 0.0 all-gather.3.cloned.1.call-start
  6.5 0.7 all-gather.3.cloned.1.call-update
  7.3 161.6 %gather.1 = (bf16[4,2,12,64,256]{4,3,2,1,0:T(8,128)(2,1)}, bf16[8,1536,512]{2,1,0:T(8,128)(2,1)}) custom-call(bf16[2,12,64,256]{3,2,1,0:T(8,128)(2,1)} %screen.1, bf16[1536,512]{1,0:T(8,128)(2,1)} %coeffs.1), custom_call_target="tpu_custom_call" | custom-call | tf_op jit(solution)/shard_map/gather/pallas_call | solution.py:130
  168.9 0.8 copy.10
  169.6 0.6 reshape.21.slots
  170.2 15.4 %pack.1 = bf16[24,2,256,256]{3,2,1,0:T(8,128)(2,1)} custom-call(s32[24]{0:T(128)} %reshape.21.slots, bf16[4,2,12,64,256]{4,3,2,1,0:T(8,128)(2,1)} %get-tuple-element.7.tile), custom_call_target="tpu_custom_call" | custom-call | tf_op jit(solution)/shard_map/pack/pallas_call | solution.py:155
  185.6 71.1 %exchange.1 = bf16[8,3,2,256,256]{4,3,2,1,0:T(8,128)(2,1)} custom-call(bf16[8,3,2,256,256]{4,3,2,1,0:T(8,128)(2,1)} %bitcast.17), custom_call_target="tpu_custom_call" | custom-call | tf_op jit(solution)/shard_map/exchange/pallas_call | solution.py:193
  257.4 21.6 %row_sums.1 = bf16[6,256,1024]{2,1,0:T(8,128)(2,1)} custom-call(s32[1]{0:T(128)S(6)} %copy.13.count, s32[24]{0:T(128)} %bitcast.20, s32[24]{0:T(128)} %bitcast.21, s32[24]{0:T(128)} %bitcast.22, bf16[2,24,256,256]{3,2,1,0:T(8,128)(2,1)} %green.1, bf16[24,2,256,256]{3,2,1,0:T(8,128)(2,1)} %bitcast.16, bf16[48,256,512]{2,1,0:T(8,128)(2,1)} %bitcast.18), custom_call_target="tpu_custom_call" | custom-call | tf_op jit(solution)/shard_map/row_sums/pallas_call | solution.py:234
  279.0 0.0 all-gather.3.cloned.1.call-done
  279.0 9.8 %convolution_convert_fusion = bf16[1024,4,512]{0,2,1:T(8,128)(2,1)S(1)} fusion(bf16[1536,1024,1]{1,0,2:T(8,128)(2,1)} %bitcast.19, bf16[4,1536,512]{2,1,0:T(8,128)(2,1)} %bitcast.23), kind=kOutput, calls=%fused_computation | convolution fusion | flops 6444548096 | bytes 13631488 | tf_op jit(solution)/shard_map/zkn,km->znm/dot_general | solution.py:327
  288.8 26.2 %scatter.1 = f32[256,1024]{1,0:T(8,128)S(1)} custom-call(bf16[8,256,1024]{2,1,0:T(8,128)(2,1)S(1)} %bitcast.15), custom_call_target="tpu_custom_call" | custom-call | tf_op jit(solution)/shard_map/scatter/pallas_call | solution.py:294
  315.0 1.9 reshape.27
Async XLA Ops:
  6.5 272.5 %all-gather.3.cloned.1.call-start = ((), (), s32[]{:S(2)}) async-start(), calls=%async_computation | async-start | bytes 7864320 | tf_op jit(solution)/shard_map/all_gather | solution.py:320
Sparse Core Ops, SparseCore 0:
  8.9 150.5 all-gather.2

commit v2 on v1

--- a/solution.py
+++ b/solution.py
@@ -31,11 +31,69 @@
     pl.semaphore_signal(barrier, inc=1, device_id=(blk, orb), device_id_type=MESH)
 
 
-def gather_kernel(n_blk, n_orb, screen, coeffs, whole, panel, local, zsend, zrecv,
-                  psend, precv, fsend, frecv):
+def line_peers(z, n_orb):
+    return jnp.minimum(z, 1) + jnp.minimum(n_orb - 1 - z, 1)
+
+
+class Line:
+    def __init__(self, n_orb, me, z, own, held, send, recv):
+        self.n_orb, self.me, self.z, self.own = n_orb, me, z, own
+        self.held, self.send, self.recv = held, send, recv
+
+    def down(self, src, block=None):
+        block = self.held.at[src] if block is None else block
+        return remote(block, self.held.at[src], self.send.at[0, src], self.recv.at[src], self.me, self.z - 1)
+
+    def up(self, src, block=None):
+        block = self.held.at[src] if block is None else block
+        return remote(block, self.held.at[src], self.send.at[1, src], self.recv.at[src], self.me, self.z + 1)
+
+    def start(self):
+        @pl.when(self.z > 0)
+        def _():
+            self.down(self.z, self.own).start()
+
+        @pl.when(self.z < self.n_orb - 1)
+        def _():
+            self.up(self.z, self.own).start()
+
+    def step(self, distance):
+        @pl.when(self.z - distance >= 0)
+        def _():
+            src = self.z - distance
+            self.up(src).wait_recv()
+
+            @pl.when(self.z < self.n_orb - 1)
+            def _():
+                self.up(src).start()
+
+        @pl.when(self.z + distance < self.n_orb)
+        def _():
+            src = self.z + distance
+            self.down(src).wait_recv()
+
+            @pl.when(self.z > 0)
+            def _():
+                self.down(src).start()
+
+    def sent(self):
+        for src in range(self.n_orb):
+            @pl.when((self.z > 0) & (src >= self.z))
+            def _():
+                self.down(src).wait_send()
+
+            @pl.when((self.z < self.n_orb - 1) & (src <= self.z))
+            def _():
+                self.up(src).wait_send()
+
+
+def spread_kernel(n_blk, n_orb, cap, slots, screen, coeffs, arrived, panel, rows, whole, packed, local, zsend,
+                  zrecv, csend, crecv, psend, precv, fsend, frecv, xsend, xrecv):
     me, z = lax.axis_index("blk"), lax.axis_index("orb")
     partner = flip(me, 1)
     masks = list(range(2, n_blk, 2))
+    order = sorted(range(1, n_blk), key=lambda mask: -bin(mask).count("1"))
+    height = screen.shape[2]
     barrier = pltpu.get_barrier_semaphore()
 
     @pl.when(z > 0)
@@ -46,23 +104,13 @@
     def _():
         greet(barrier, me, z + 1)
 
-    for mask in [1] + masks:
+    for mask in range(1, n_blk):
         greet(barrier, flip(me, mask), z)
-    pl.semaphore_wait(barrier, len(masks) + 1 + jnp.minimum(z, 1) + jnp.minimum(n_orb - 1 - z, 1))
-
-    def down(src, block):
-        return remote(block, whole.at[src], zsend.at[0, src], zrecv.at[src], me, z - 1)
-
-    def up(src, block):
-        return remote(block, whole.at[src], zsend.at[1, src], zrecv.at[src], me, z + 1)
-
-    @pl.when(z > 0)
-    def _():
-        down(z, screen).start()
-
-    @pl.when(z < n_orb - 1)
-    def _():
-        up(z, screen).start()
+    pl.semaphore_wait(barrier, n_blk - 1 + line_peers(z, n_orb))
+
+    tiles = Line(n_orb, me, z, screen, whole, zsend, zrecv)
+    points = Line(n_orb, me, z, coeffs, rows, csend, crecv)
+    tiles.start()
 
     def direct(mask):
         return remote(coeffs, panel.at[me], psend.at[mask // 2], precv.at[mask // 2], flip(me, mask), z)
@@ -78,127 +126,85 @@
     forward(0).start()
     own_screen = pltpu.make_async_copy(screen, whole.at[z], local.at[0])
     own_coeffs = pltpu.make_async_copy(coeffs, panel.at[me], local.at[1])
+    own_points = pltpu.make_async_copy(coeffs, rows.at[z], local.at[2])
     own_screen.start()
     own_coeffs.start()
-
-    for step in range(1, max(n_orb, len(masks) + 1)):
-        if step < n_orb:
-            @pl.when(z - step >= 0)
-            def _():
-                src = z - step
-                up(src, whole.at[src]).wait_recv()
-
-                @pl.when(z < n_orb - 1)
-                def _():
-                    up(src, whole.at[src]).start()
-
-            @pl.when(z + step < n_orb)
-            def _():
-                src = z + step
-                down(src, whole.at[src]).wait_recv()
-
-                @pl.when(z > 0)
-                def _():
-                    down(src, whole.at[src]).start()
-        if step - 1 < len(masks):
-            mask = masks[step - 1]
-            owner = flip(me, mask)
-            remote(coeffs, panel.at[owner], psend.at[mask // 2], precv.at[mask // 2], owner, z).wait_recv()
-            forward(mask).start()
-
+    own_points.start()
+    for distance in range(1, n_orb):
+        tiles.step(distance)
     own_screen.wait()
+    tiles.sent()
+    points.start()
+
+    def fill(peer):
+        def one(c, unused):
+            slot = slots[peer * cap + c]
+            for q in range(n_orb):
+                packed[peer, c, :, q * height:(q + 1) * height, :] = whole[q, :, slot]
+            return unused
+
+        lax.fori_loop(0, cap, one, 0)
+
+    def deliver(mask):
+        peer = flip(me, mask)
+        return remote(packed.at[peer], arrived.at[me], xsend.at[mask], xrecv.at[mask], peer, z)
+
+    for mask in order:
+        fill(flip(me, mask))
+        deliver(mask).start()
+    fill(me)
+    own_tiles = pltpu.make_async_copy(packed.at[me], arrived.at[me], local.at[3])
+    own_tiles.start()
+
+    for mask in masks:
+        owner = flip(me, mask)
+        remote(coeffs, panel.at[owner], psend.at[mask // 2], precv.at[mask // 2], owner, z).wait_recv()
+        forward(mask).start()
+    for distance in range(1, n_orb):
+        points.step(distance)
+
     own_coeffs.wait()
+    own_points.wait()
+    own_tiles.wait()
     for mask in masks:
         direct(mask).wait_send()
     for mask in [0] + masks:
         forward(mask).wait_send()
         owner = flip(partner, mask)
         remote(coeffs, panel.at[owner], fsend.at[mask // 2], frecv.at[mask // 2], partner, z).wait_recv()
-
-    for src in range(n_orb):
-        @pl.when((z > 0) & (src >= z))
-        def _():
-            down(src, whole.at[src]).wait_send()
-
-        @pl.when((z < n_orb - 1) & (src <= z))
-        def _():
-            up(src, whole.at[src]).wait_send()
-
-
-def gather(screen, coeffs, n_blk, n_orb):
+    for mask in order:
+        deliver(mask).wait_send()
+        peer = flip(me, mask)
+        remote(packed.at[peer], arrived.at[peer], xsend.at[mask], xrecv.at[mask], peer, z).wait_recv()
+    points.sent()
+
+
+def spread(screen, coeffs, outgoing, n_blk, n_orb):
     dma = pltpu.SemaphoreType.DMA
+    times, _, height, width = screen.shape
+    cap = outgoing.shape[0] // n_blk
+    tiles = (n_blk, cap, times, n_orb * height, width)
+    half = n_blk // 2
     return pl.pallas_call(
-        functools.partial(gather_kernel, n_blk, n_orb),
+        functools.partial(spread_kernel, n_blk, n_orb, cap),
         out_shape=(
-            jax.ShapeDtypeStruct((n_orb,) + screen.shape, screen.dtype),
+            jax.ShapeDtypeStruct(tiles, screen.dtype),
             jax.ShapeDtypeStruct((n_blk,) + coeffs.shape, coeffs.dtype),
-        ),
-        in_specs=[ANY, ANY],
-        out_specs=(ANY, ANY),
+            jax.ShapeDtypeStruct((n_orb,) + coeffs.shape, coeffs.dtype),
+        ),
+        in_specs=[pl.BlockSpec(memory_space=pltpu.SMEM), ANY, ANY],
+        out_specs=(ANY, ANY, ANY),
         scratch_shapes=[
-            dma((2,)), dma((2, n_orb)), dma((n_orb,)),
-            dma((n_blk // 2,)), dma((n_blk // 2,)), dma((n_blk // 2,)), dma((n_blk // 2,)),
+            pltpu.VMEM((n_orb,) + screen.shape, screen.dtype),
+            pltpu.VMEM(tiles, screen.dtype),
+            dma((4,)), dma((2, n_orb)), dma((n_orb,)), dma((2, n_orb)), dma((n_orb,)),
+            dma((half,)), dma((half,)), dma((half,)), dma((half,)), dma((n_blk,)), dma((n_blk,)),
         ],
-        compiler_params=pltpu.CompilerParams(collective_id=1, has_side_effects=True),
-        name="gather",
-    )(screen, coeffs)
-
-
-def pack(whole, outgoing):
-    n_orb, times, _, rows, width = whole.shape
-    total = outgoing.shape[0]
-
-    def body(slots, tile, out):
-        for q in range(n_orb):
-            out[0, :, q * rows:(q + 1) * rows, :] = tile[q, :, 0]
-
-    return pl.pallas_call(
-        body,
-        out_shape=jax.ShapeDtypeStruct((total, times, n_orb * rows, width), whole.dtype),
-        grid_spec=pltpu.PrefetchScalarGridSpec(
-            num_scalar_prefetch=1,
-            grid=(total,),
-            in_specs=[pl.BlockSpec((n_orb, times, 1, rows, width), lambda j, slots: (0, 0, slots[j], 0, 0))],
-            out_specs=pl.BlockSpec((1, times, n_orb * rows, width), lambda j, slots: (j, 0, 0, 0)),
-        ),
-        name="pack",
-    )(outgoing, whole)
-
-
-def exchange_kernel(n_blk, packed, arrived, local, send, recv):
-    me, z = lax.axis_index("blk"), lax.axis_index("orb")
-    barrier = pltpu.get_barrier_semaphore()
-    for mask in range(1, n_blk):
-        greet(barrier, flip(me, mask), z)
-    pl.semaphore_wait(barrier, n_blk - 1)
-
-    def copy(mask):
-        peer = flip(me, mask)
-        return remote(packed.at[peer], arrived.at[me], send.at[mask], recv.at[mask], peer, z)
-
-    order = sorted(range(1, n_blk), key=lambda mask: -bin(mask).count("1"))
-    for mask in order:
-        copy(mask).start()
-    own = pltpu.make_async_copy(packed.at[me], arrived.at[me], local)
-    own.start()
-    own.wait()
-    for mask in order:
-        copy(mask).wait_send()
-        peer = flip(me, mask)
-        remote(packed.at[peer], arrived.at[peer], send.at[mask], recv.at[mask], peer, z).wait_recv()
-
-
-def exchange(packed, n_blk):
-    dma = pltpu.SemaphoreType.DMA
-    return pl.pallas_call(
-        functools.partial(exchange_kernel, n_blk),
-        out_shape=jax.ShapeDtypeStruct(packed.shape, packed.dtype),
-        in_specs=[ANY],
-        out_specs=ANY,
-        scratch_shapes=[dma, dma((n_blk,)), dma((n_blk,))],
-        compiler_params=pltpu.CompilerParams(collective_id=2, has_side_effects=True),
-        name="exchange",
-    )(packed)
+        compiler_params=pltpu.CompilerParams(
+            collective_id=1, has_side_effects=True, vmem_limit_bytes=56 * 2**20
+        ),
+        name="spread",
+    )(outgoing, screen, coeffs)
 
 
 def rows_kernel(count, codes, targets, columns, green, screen, block, out, acc):
@@ -316,12 +322,9 @@
     times, _, width, _ = green_tiles.shape
     owned = coeffs.shape[0] // width
     orbitals = coeffs.shape[1]
-    whole, panel = gather(screen_tiles, coeffs, n_blk, n_orb)
-    own_rows = lax.all_gather(coeffs, "orb", axis=0)
-    packed = pack(whole, send_slot.reshape(-1))
-    arrived = exchange(packed.reshape((n_blk, -1) + packed.shape[1:]), n_blk)
+    arrived, panel, own_rows = spread(screen_tiles, coeffs, send_slot.reshape(-1), n_blk, n_orb)
     folded = row_sums(
-        green_tiles, arrived.reshape(packed.shape), panel.reshape(-1, width, orbitals),
+        green_tiles, arrived.reshape((-1,) + arrived.shape[2:]), panel.reshape(-1, width, orbitals),
         tile_count, recv_index[0], row_block[0], col_block[0], owned,
     ).reshape(owned * width, times * orbitals)
     part = jnp.einsum("zkn,km->znm", own_rows, folded, preferred_element_type=jnp.float32)

time: 325 us -> 224 us (0.69)
  Pallas kernels: 296 us -> 213 us
  between operations: 14.1 us -> 0.69 us
    pallas_call x3 -> x1, Pallas kernels: 248 us -> 164 us  [spread(): pl.pallas_call(functools.partial(spread_kernel, n_blk, n_orb, cap), out_s...]
  transfers between devices with their start and end apart: 1 -> 0, of which waited for: 0 -> 0; matrix products, arithmetic and copies ran while one was open for 0% -> 0% of each run, Pallas kernels for 83% -> 0%
where the time goes in v2:
time: 224 us; the launch traced here: 226 us
  Pallas kernels  213 us (95%)
  matrix products  8.37 us (4%)
  local copies, waits for them, and re-layouts  3.21 us (1%)
    pallas_call x1, Pallas kernels, spread(): pl.pallas_call(functools.partial(spread_kernel, n_blk, n_orb, cap), out_s...  164 us
    pallas_call x1, Pallas kernels, scatter(): pl.pallas_call(functools.partial(scatter_kernel, n_blk), out_shape=jax.Sh...  27.6 us
    pallas_call x1, Pallas kernels, row_sums(): pl.pallas_call(rows_kernel, out_shape=jax.ShapeDtypeStruct((owned, width,...  21.6 us
    dot_general x1, matrix products, shards(): jnp.einsum('zkn,km->znm', own_rows, folded, preferred_element_type=jnp.fl...  8.37 us

profile of v2, /device:TPU:0, one launch (start us, length us, event | category | flops | bytes accessed | tf_op | source)
XLA Modules:
  0.0 225.6 jit_solution(5245149951836048208)
XLA Ops:
  0.7 0.8 copy.11
  1.4 0.6 reshape.18.slots
  2.0 164.1 %spread.1 = (bf16[8,3,2,256,256]{4,3,2,1,0:T(8,128)(2,1)}, bf16[8,1536,512]{2,1,0:T(8,128)(2,1)}, bf16[4,1536,512]{2,1,0:T(8,128)(2,1)}) custom-call(s32[24]{0:T(128)} %reshape.18.slots, bf16[2,12,64,256]{3,2,1,0:T(8,128)(2,1)} %screen.1, bf16[1536,512]{1,0:T(8,128)(2,1)} %coeffs.1), custom_call_target="tpu_custom_call" | custom-call | tf_op jit(solution)/shard_map/spread/pallas_call | solution.py:188
  166.1 0.0 copy-start
  166.2 21.6 %row_sums.1 = bf16[6,256,1024]{2,1,0:T(8,128)(2,1)} custom-call(s32[1]{0:T(128)S(6)} %copy.14.count, s32[24]{0:T(128)} %bitcast.15, s32[24]{0:T(128)} %bitcast.16, s32[24]{0:T(128)} %bitcast.17, bf16[2,24,256,256]{3,2,1,0:T(8,128)(2,1)} %green.1, bf16[24,2,256,256]{3,2,1,0:T(8,128)(2,1)} %bitcast.13, bf16[48,256,512]{2,1,0:T(8,128)(2,1)} %bitcast.12), custom_call_target="tpu_custom_call" | custom-call | tf_op jit(solution)/shard_map/row_sums/pallas_call | solution.py:240
  187.7 0.0 copy-done
  187.7 8.4 %convolution_convert_fusion = bf16[4,512,1024]{2,1,0:T(8,128)(2,1)S(1)} fusion(bf16[4,1536,512]{2,1,0:T(8,128)(2,1)S(1)} %copy-done, bf16[1536,1024,1]{1,0,2:T(8,128)(2,1)} %bitcast.14), kind=kOutput, calls=%fused_computation | convolution fusion | flops 6444548096 | bytes 13631488 | tf_op jit(solution)/shard_map/zkn,km->znm/dot_general | solution.py:330
  196.1 27.6 %scatter.1 = f32[256,1024]{1,0:T(8,128)S(1)} custom-call(bf16[8,256,1024]{2,1,0:T(8,128)(2,1)S(1)} %bitcast.11), custom_call_target="tpu_custom_call" | custom-call | tf_op jit(solution)/shard_map/scatter/pallas_call | solution.py:300
  223.8 1.9 reshape.23
Async XLA Ops:
  166.1 21.6 %copy-start = (bf16[4,1536,512]{2,1,0:T(8,128)(2,1)S(1)}, bf16[4,1536,512]{2,1,0:T(8,128)(2,1)}, u32[]{:S(2)}) copy-start(bf16[4,1536,512]{2,1,0:T(8,128)(2,1)} %get-tuple-element.8) | copy-start | bytes 18874372

commit v3 on v2

--- a/solution.py
+++ b/solution.py
@@ -88,10 +88,13 @@
 
 
 def spread_kernel(n_blk, n_orb, cap, slots, screen, coeffs, arrived, panel, rows, whole, packed, local, zsend,
-                  zrecv, csend, crecv, psend, precv, fsend, frecv, xsend, xrecv):
+                  zrecv, csend, crecv, psend, precv, fsend, frecv, xsend, xrecv, rsend, rrecv):
     me, z = lax.axis_index("blk"), lax.axis_index("orb")
     partner = flip(me, 1)
     masks = list(range(2, n_blk, 2))
+    relayed = [mask for mask in masks if bin(mask).count("1") == 2]
+    plain = [mask for mask in masks if mask not in relayed]
+    part = coeffs.shape[0] // 2
     order = sorted(range(1, n_blk), key=lambda mask: -bin(mask).count("1"))
     height = screen.shape[2]
     barrier = pltpu.get_barrier_semaphore()
@@ -115,8 +118,18 @@
     def direct(mask):
         return remote(coeffs, panel.at[me], psend.at[mask // 2], precv.at[mask // 2], flip(me, mask), z)
 
-    for mask in masks:
+    for mask in plain:
         direct(mask).start()
+
+    def relay(mask, i):
+        low = mask & -mask
+        via = (low, mask - low)[i]
+        block = panel.at[flip(me, mask - via), pl.ds(i * part, part)]
+        return remote(block, block, rsend.at[i, mask // 2], rrecv.at[i, mask // 2], flip(me, via), z)
+
+    def relay_arrives(mask, i):
+        block = panel.at[flip(me, mask), pl.ds(i * part, part)]
+        remote(block, block, rsend.at[i, mask // 2], rrecv.at[i, mask // 2], partner, z).wait_recv()
 
     def forward(mask):
         owner = flip(me, mask)
@@ -131,6 +144,15 @@
     own_coeffs.start()
     own_points.start()
     for distance in range(1, n_orb):
+        if distance == n_orb - 1:
+            for mask in plain:
+                owner = flip(me, mask)
+                remote(coeffs, panel.at[owner], psend.at[mask // 2], precv.at[mask // 2], owner, z).wait_recv()
+            for mask in relayed:
+                relay(mask, 0).start()
+                relay(mask, 1).start()
+            for mask in plain:
+                forward(mask).start()
         tiles.step(distance)
     own_screen.wait()
     tiles.sent()
@@ -156,9 +178,9 @@
     own_tiles = pltpu.make_async_copy(packed.at[me], arrived.at[me], local.at[3])
     own_tiles.start()
 
-    for mask in masks:
-        owner = flip(me, mask)
-        remote(coeffs, panel.at[owner], psend.at[mask // 2], precv.at[mask // 2], owner, z).wait_recv()
+    for mask in relayed:
+        relay_arrives(mask, 0)
+        relay_arrives(mask, 1)
         forward(mask).start()
     for distance in range(1, n_orb):
         points.step(distance)
@@ -166,8 +188,11 @@
     own_coeffs.wait()
     own_points.wait()
     own_tiles.wait()
-    for mask in masks:
+    for mask in plain:
         direct(mask).wait_send()
+    for mask in relayed:
+        relay(mask, 0).wait_send()
+        relay(mask, 1).wait_send()
     for mask in [0] + masks:
         forward(mask).wait_send()
         owner = flip(partner, mask)
@@ -199,6 +224,7 @@
             pltpu.VMEM(tiles, screen.dtype),
             dma((4,)), dma((2, n_orb)), dma((n_orb,)), dma((2, n_orb)), dma((n_orb,)),
             dma((half,)), dma((half,)), dma((half,)), dma((half,)), dma((n_blk,)), dma((n_blk,)),
+            dma((2, half)), dma((2, half)),
         ],
         compiler_params=pltpu.CompilerParams(
             collective_id=1, has_side_effects=True, vmem_limit_bytes=56 * 2**20
@@ -207,24 +233,32 @@
     )(outgoing, screen, coeffs)
 
 
-def rows_kernel(count, codes, targets, columns, green, screen, block, out, acc):
-    slot = pl.program_id(0)
-    orbitals = block.shape[2]
-
-    @pl.when(slot == 0)
+GROUP = 4
+
+
+def rows_kernel(count, codes, targets, columns, *refs):
+    step = pl.program_id(0)
+    greens, screens, blocks = (refs[i * GROUP:(i + 1) * GROUP] for i in range(3))
+    out, acc = refs[3 * GROUP:]
+    orbitals = blocks[0].shape[2]
+
+    @pl.when(step == 0)
     def _():
         acc[...] = jnp.zeros_like(acc)
 
-    @pl.when(slot < count[0])
-    def _():
-        target = targets[slot]
-        for t in range(green.shape[0]):
-            sigma = (-(green[t, 0].astype(jnp.float32) * screen[0, t].astype(jnp.float32))).astype(jnp.bfloat16)
-            acc[target, :, t * orbitals:(t + 1) * orbitals] += jnp.dot(
-                sigma, block[0], preferred_element_type=jnp.float32
-            )
-
-    @pl.when(slot == pl.num_programs(0) - 1)
+    for g in range(GROUP):
+        slot = step * GROUP + g
+
+        @pl.when(slot < count[0])
+        def _():
+            target = targets[slot]
+            for t in range(greens[g].shape[0]):
+                sigma = -(greens[g][t, 0].astype(jnp.float32) * screens[g][0, t].astype(jnp.float32))
+                acc[target, :, t * orbitals:(t + 1) * orbitals] += jnp.dot(
+                    sigma.astype(jnp.bfloat16), blocks[g][0], preferred_element_type=jnp.float32
+                )
+
+    @pl.when(step == pl.num_programs(0) - 1)
     def _():
         for i in range(acc.shape[0]):
             out[i] = acc[i].astype(out.dtype)
@@ -234,86 +268,107 @@
     times, slots, width, _ = green.shape
     orbitals = blocks.shape[2]
 
-    def live(s, count):
-        return jnp.minimum(s, count[0] - 1)
-
+    def live(s, g, count):
+        return jnp.minimum(s * GROUP + g, count[0] - 1)
+
+    def green_spec(g):
+        return pl.BlockSpec((times, 1, width, width), lambda s, n, c, r, k: (0, live(s, g, n), 0, 0))
+
+    def screen_spec(g):
+        return pl.BlockSpec((1, times, width, width), lambda s, n, c, r, k: (c[live(s, g, n)], 0, 0, 0))
+
+    def block_spec(g):
+        return pl.BlockSpec((1, width, orbitals), lambda s, n, c, r, k: (k[live(s, g, n)], 0, 0))
+
+    specs = [spec(g) for spec in (green_spec, screen_spec, block_spec) for g in range(GROUP)]
     return pl.pallas_call(
         rows_kernel,
         out_shape=jax.ShapeDtypeStruct((owned, width, times * orbitals), jnp.bfloat16),
         grid_spec=pltpu.PrefetchScalarGridSpec(
             num_scalar_prefetch=4,
-            grid=(slots,),
-            in_specs=[
-                pl.BlockSpec((times, 1, width, width), lambda s, n, c, r, k: (0, live(s, n), 0, 0)),
-                pl.BlockSpec((1, times, width, width), lambda s, n, c, r, k: (c[live(s, n)], 0, 0, 0)),
-                pl.BlockSpec((1, width, orbitals), lambda s, n, c, r, k: (k[live(s, n)], 0, 0)),
-            ],
+            grid=(slots // GROUP,),
+            in_specs=specs,
             out_specs=pl.BlockSpec((owned, width, times * orbitals), lambda s, n, c, r, k: (0, 0, 0)),
             scratch_shapes=[pltpu.VMEM((owned, width, times * orbitals), jnp.float32)],
         ),
         compiler_params=pltpu.CompilerParams(vmem_limit_bytes=56 * 2**20),
         name="row_sums",
-    )(count, codes, targets, columns, green, arrived, blocks)
-
-
-def scatter_kernel(n_blk, part, out, first, second, stage, total, ssend, srecv, send, recv):
+    )(count, codes, targets, columns, *([green] * GROUP + [arrived] * GROUP + [blocks] * GROUP))
+
+
+def scatter_kernel(n_blk, points, sums, out, mine, leaving, first, second, stage, ssend, srecv, send, recv):
     me, z = lax.axis_index("blk"), lax.axis_index("orb")
     partner = flip(me, 1)
     masks = sorted(range(2, n_blk, 2), key=lambda mask: -bin(mask).count("1"))
+    rows = out.shape[0]
+    per = points.shape[2] // rows
     barrier = pltpu.get_barrier_semaphore()
     for mask in [1] + masks:
         greet(barrier, flip(me, mask), z)
     pl.semaphore_wait(barrier, len(masks) + 1)
 
+    def chunk(owner):
+        start = pl.multiple_of(lax.rem(owner, per) * rows, rows)
+        return lax.dot_general(
+            points[lax.div(owner, per), :, pl.ds(start, rows)], sums[...], (((0,), (0,)), ((), ())),
+            preferred_element_type=jnp.float32,
+        )
+
     def to_partner(mask):
         h = mask // 2
-        return remote(part.at[flip(partner, mask)], first.at[h], ssend.at[h], srecv.at[h], partner, z)
+        return remote(leaving.at[h], first.at[h], ssend.at[h], srecv.at[h], partner, z)
 
     def to_owner(mask):
         h = mask // 2
         return remote(stage.at[h], second.at[h], send.at[h], recv.at[h], flip(me, mask), z)
 
-    for mask in masks + [0]:
-        to_partner(mask).start()
-    for mask in masks:
+    def finish(mask):
         h = mask // 2
         to_partner(mask).wait_recv()
-        stage[h] = (part[flip(me, mask)].astype(jnp.float32) + first[h].astype(jnp.float32)).astype(stage.dtype)
-        to_owner(mask).start()
-    to_partner(0).wait_recv()
-    total[...] = part[me].astype(jnp.float32) + first[0].astype(jnp.float32)
+        if mask:
+            stage[h] = (mine[h] + first[h].astype(jnp.float32)).astype(stage.dtype)
+            to_owner(mask).start()
+        else:
+            out[...] = mine[h] + first[h].astype(jnp.float32)
+
+    turns = masks + [0]
+    for i, mask in enumerate(turns):
+        h = mask // 2
+        leaving[h] = chunk(flip(partner, mask)).astype(leaving.dtype)
+        to_partner(mask).start()
+        mine[h] = chunk(flip(me, mask))
+        if i:
+            finish(turns[i - 1])
+    finish(0)
     for mask in masks[::-1]:
         to_owner(mask).wait_recv()
-        total[...] += second[mask // 2].astype(jnp.float32)
-    out[...] = total[...]
-    for mask in masks + [0]:
+        out[...] += second[mask // 2].astype(jnp.float32)
+    for mask in turns:
         to_partner(mask).wait_send()
     for mask in masks:
         to_owner(mask).wait_send()
 
 
-def scatter(part):
-    n_blk, rows, columns = part.shape
+def scatter(points, sums, n_blk):
+    rows, columns = points.shape[0] * points.shape[2] // n_blk, sums.shape[1]
     half = n_blk // 2
     dma = pltpu.SemaphoreType.DMA
     vmem = pl.BlockSpec(memory_space=pltpu.VMEM)
+    chunks = pltpu.VMEM((half, rows, columns), jnp.bfloat16)
     return pl.pallas_call(
         functools.partial(scatter_kernel, n_blk),
         out_shape=jax.ShapeDtypeStruct((rows, columns), jnp.float32),
-        in_specs=[vmem],
+        in_specs=[vmem, vmem],
         out_specs=vmem,
         scratch_shapes=[
-            pltpu.VMEM((half, rows, columns), jnp.bfloat16),
-            pltpu.VMEM((half, rows, columns), jnp.bfloat16),
-            pltpu.VMEM((half, rows, columns), jnp.bfloat16),
-            pltpu.VMEM((rows, columns), jnp.float32),
+            pltpu.VMEM((half, rows, columns), jnp.float32), chunks, chunks, chunks, chunks,
             dma((half,)), dma((half,)), dma((half,)), dma((half,)),
         ],
         compiler_params=pltpu.CompilerParams(
-            collective_id=3, has_side_effects=True, vmem_limit_bytes=32 * 2**20
+            collective_id=3, has_side_effects=True, vmem_limit_bytes=48 * 2**20
         ),
         name="scatter",
-    )(part)
+    )(points, sums)
 
 
 def shards(
@@ -327,9 +382,7 @@
         green_tiles, arrived.reshape((-1,) + arrived.shape[2:]), panel.reshape(-1, width, orbitals),
         tile_count, recv_index[0], row_block[0], col_block[0], owned,
     ).reshape(owned * width, times * orbitals)
-    part = jnp.einsum("zkn,km->znm", own_rows, folded, preferred_element_type=jnp.float32)
-    part = part.astype(jnp.bfloat16).reshape(n_blk, -1, times * orbitals)
-    return scatter(part).reshape(-1, times, orbitals)
+    return scatter(own_rows, folded, n_blk).reshape(-1, times, orbitals)
 
 
 def solution(mesh):

time: 224 us -> 216 us (0.964)
  matrix products: 8.37 us -> 0 us
    pallas_call x1, Pallas kernels: 21.6 us -> 7.38 us  [row_sums(): pl.pallas_call(rows_kernel, out_shape=jax.ShapeDtypeStruct((owned, width,...]
    pallas_call x1, Pallas kernels: 27.6 us -> 39.3 us  [scatter(): pl.pallas_call(functools.partial(scatter_kernel, n_blk), out_shape=jax.Sh...]
    dot_general x1 -> x0, matrix products: 8.37 us -> none  [shards(): jnp.einsum('zkn,km->znm', own_rows, folded, preferred_element_type=jnp.fl...]
where the time goes in v3:
time: 216 us
  Pallas kernels  211 us (98%)
  local copies, waits for them, and re-layouts  5.09 us (2%)
    pallas_call x1, Pallas kernels, spread(): pl.pallas_call(functools.partial(spread_kernel, n_blk, n_orb, cap), out_s...  164 us
    pallas_call x1, Pallas kernels, scatter(): pl.pallas_call(functools.partial(scatter_kernel, n_blk), out_shape=jax.Sh...  39.3 us
    pallas_call x1, Pallas kernels, row_sums(): pl.pallas_call(rows_kernel, out_shape=jax.ShapeDtypeStruct((owned, width,...  7.38 us

profile of v3, /device:TPU:0, one launch (start us, length us, event | category | flops | bytes accessed | tf_op | source)
XLA Modules:
  0.0 216.3 jit_solution(10092046591982506279)
XLA Ops:
  0.7 0.8 copy.10
  1.4 0.6 reshape.15.slots
  2.0 163.8 %spread.1 = (bf16[8,3,2,256,256]{4,3,2,1,0:T(8,128)(2,1)}, bf16[8,1536,512]{2,1,0:T(8,128)(2,1)}, bf16[4,1536,512]{2,1,0:T(8,128)(2,1)}) custom-call(s32[24]{0:T(128)} %reshape.15.slots, bf16[2,12,64,256]{3,2,1,0:T(8,128)(2,1)} %screen.1, bf16[1536,512]{1,0:T(8,128)(2,1)} %coeffs.1), custom_call_target="tpu_custom_call" | custom-call | tf_op jit(solution)/shard_map/spread/pallas_call | solution.py:213
  165.8 7.4 %row_sums.1 = bf16[6,256,1024]{2,1,0:T(8,128)(2,1)} custom-call(s32[1]{0:T(128)S(6)} %copy.11.count, s32[24]{0:T(128)} %bitcast.15, s32[24]{0:T(128)} %bitcast.16, s32[24]{0:T(128)} %bitcast.17, bf16[2,24,256,256]{3,2,1,0:T(8,128)(2,1)} %refs_3_.1, bf16[2,24,256,256]{3,2,1,0:T(8,128)(2,1)} %refs_3_.1, bf16[2,24,256,256]{3,2,1,0:T(8,128)(2,1)} %refs_3_.1, ...), custom_call_target="tpu_custom_call" | custom-call | tf_op jit(solution)/shard_map/row_sums/pallas_call | solution.py:284
  173.2 0.0 copy-start
  173.2 1.9 copy-done
  175.1 39.3 %scatter.1 = f32[256,1024]{1,0:T(8,128)S(1)} custom-call(bf16[4,1536,512]{2,1,0:T(8,128)(2,1)} %get-tuple-element.8.points, bf16[1536,1024]{1,0:T(8,128)(2,1)S(1)} %bitcast.6), custom_call_target="tpu_custom_call" | custom-call | tf_op jit(solution)/shard_map/scatter/pallas_call | solution.py:358
  214.4 1.9 reshape.19
Async XLA Ops:
  173.2 1.9 copy-start

commit v4 on v3

--- a/solution.py
+++ b/solution.py
@@ -75,6 +75,19 @@
             @pl.when(self.z > 0)
             def _():
                 self.down(src).start()
+
+    def then(self, turn, following):
+        @pl.when((self.z == turn) & (self.z < self.n_orb - 1))
+        def _():
+            for src in range(turn + 1):
+                self.up(src).wait_send()
+            following.up(self.z, following.own).start()
+
+        @pl.when((self.z == self.n_orb - 1 - turn) & (self.z > 0))
+        def _():
+            for src in range(self.n_orb - 1 - turn, self.n_orb):
+                self.down(src).wait_send()
+            following.down(self.z, following.own).start()
 
     def sent(self):
         for src in range(self.n_orb):
@@ -153,10 +166,9 @@
                 relay(mask, 1).start()
             for mask in plain:
                 forward(mask).start()
+        tiles.then(distance - 1, points)
         tiles.step(distance)
     own_screen.wait()
-    tiles.sent()
-    points.start()
 
     def fill(peer):
         def one(c, unused):
@@ -291,7 +303,7 @@
             out_specs=pl.BlockSpec((owned, width, times * orbitals), lambda s, n, c, r, k: (0, 0, 0)),
             scratch_shapes=[pltpu.VMEM((owned, width, times * orbitals), jnp.float32)],
         ),
-        compiler_params=pltpu.CompilerParams(vmem_limit_bytes=56 * 2**20),
+        compiler_params=pltpu.CompilerParams(vmem_limit_bytes=46 * 2**20),
         name="row_sums",
     )(count, codes, targets, columns, *([green] * GROUP + [arrived] * GROUP + [blocks] * GROUP))
 

time: 216 us -> 213 us (0.986)
  Pallas kernels: 211 us -> 208 us
    pallas_call x1, Pallas kernels: 39.3 us -> 34.3 us  [scatter(): pl.pallas_call(functools.partial(scatter_kernel, n_blk), out_shape=jax.Sh...]
    pallas_call x1, Pallas kernels: 7.38 us -> 9.98 us  [row_sums(): pl.pallas_call(rows_kernel, out_shape=jax.ShapeDtypeStruct((owned, width,...]
where the time goes in v4:
time: 213 us; the launch traced here: 214 us
  Pallas kernels  208 us (98%)
  local copies, waits for them, and re-layouts  5.17 us (2%)
    pallas_call x1, Pallas kernels, spread(): pl.pallas_call(functools.partial(spread_kernel, n_blk, n_orb, cap), out_s...  164 us
    pallas_call x1, Pallas kernels, scatter(): pl.pallas_call(functools.partial(scatter_kernel, n_blk), out_shape=jax.Sh...  34.3 us
    pallas_call x1, Pallas kernels, row_sums(): pl.pallas_call(rows_kernel, out_shape=jax.ShapeDtypeStruct((owned, width,...  9.98 us

profile of v4, /device:TPU:0, one launch (start us, length us, event | category | flops | bytes accessed | tf_op | source)
XLA Modules:
  0.0 213.9 jit_solution(15071643906111646162)
XLA Ops:
  0.7 0.8 copy.10
  1.4 0.6 reshape.15.slots
  2.0 163.8 %spread.1 = (bf16[8,3,2,256,256]{4,3,2,1,0:T(8,128)(2,1)}, bf16[8,1536,512]{2,1,0:T(8,128)(2,1)}, bf16[4,1536,512]{2,1,0:T(8,128)(2,1)}) custom-call(s32[24]{0:T(128)} %reshape.15.slots, bf16[2,12,64,256]{3,2,1,0:T(8,128)(2,1)} %screen.1, bf16[1536,512]{1,0:T(8,128)(2,1)} %coeffs.1), custom_call_target="tpu_custom_call" | custom-call | tf_op jit(solution)/shard_map/spread/pallas_call | solution.py:225
  165.8 0.0 copy-start
  165.8 0.6 copy-done
  166.5 0.0 copy-start.1
  166.5 0.7 copy-done.1
  167.2 0.0 copy-start.2
  167.2 0.7 copy-done.2
  167.8 10.0 %row_sums.1 = bf16[6,256,1024]{2,1,0:T(8,128)(2,1)S(1)} custom-call(s32[1]{0:T(128)S(6)} %copy.11.count, s32[24]{0:T(128)S(1)} %bitcast.7, s32[24]{0:T(128)S(1)} %bitcast.8, s32[24]{0:T(128)S(1)} %bitcast.9, bf16[2,24,256,256]{3,2,1,0:T(8,128)(2,1)} %refs_3_.1, bf16[2,24,256,256]{3,2,1,0:T(8,128)(2,1)} %refs_3_.1, bf16[2,24,256,256]{3,2,1,0:T(8,128)(2,1)} %refs_3_.1, ...), custom_call_target="tpu_custom_call" | custom-call | tf_op jit(solution)/shard_map/row_sums/pallas_call | solution.py:296
  177.8 34.3 %scatter.1 = f32[256,1024]{1,0:T(8,128)S(1)} custom-call(bf16[4,1536,512]{2,1,0:T(8,128)(2,1)} %get-tuple-element.8.points, bf16[1536,1024]{1,0:T(8,128)(2,1)S(1)} %bitcast.6), custom_call_target="tpu_custom_call" | custom-call | tf_op jit(solution)/shard_map/scatter/pallas_call | solution.py:370
  212.1 1.9 reshape.19
Async XLA Ops:
  165.8 0.7 copy-start
  166.5 0.7 copy-start.1
  167.2 0.7 copy-start.2

commit v5 on v4

--- a/solution.py
+++ b/solution.py
@@ -344,14 +344,17 @@
             out[...] = mine[h] + first[h].astype(jnp.float32)
 
     turns = masks + [0]
+
+    def leave(mask):
+        leaving[mask // 2] = chunk(flip(partner, mask)).astype(leaving.dtype)
+        to_partner(mask).start()
+
+    leave(turns[0])
     for i, mask in enumerate(turns):
-        h = mask // 2
-        leaving[h] = chunk(flip(partner, mask)).astype(leaving.dtype)
-        to_partner(mask).start()
-        mine[h] = chunk(flip(me, mask))
-        if i:
-            finish(turns[i - 1])
-    finish(0)
+        mine[mask // 2] = chunk(flip(me, mask))
+        if i + 1 < len(turns):
+            leave(turns[i + 1])
+        finish(mask)
     for mask in masks[::-1]:
         to_owner(mask).wait_recv()
         out[...] += second[mask // 2].astype(jnp.float32)

time: 213 us -> 212 us (level)
    pallas_call x1, Pallas kernels: 9.98 us -> 6.08 us  [row_sums(): pl.pallas_call(rows_kernel, out_shape=jax.ShapeDtypeStruct((owned, width,...]
where the time goes in v5:
time: 212 us
  Pallas kernels  206 us (97%)
  local copies, waits for them, and re-layouts  5.17 us (2%)
    pallas_call x1, Pallas kernels, spread(): pl.pallas_call(functools.partial(spread_kernel, n_blk, n_orb, cap), out_s...  164 us
    pallas_call x1, Pallas kernels, scatter(): pl.pallas_call(functools.partial(scatter_kernel, n_blk), out_shape=jax.Sh...  36.3 us
    pallas_call x1, Pallas kernels, row_sums(): pl.pallas_call(rows_kernel, out_shape=jax.ShapeDtypeStruct((owned, width,...  6.08 us

profile of v5, /device:TPU:0, one launch (start us, length us, event | category | flops | bytes accessed | tf_op | source)
XLA Modules:
  0.0 212.1 jit_solution(2554274389447987942)
XLA Ops:
  0.7 0.8 copy.10
  1.4 0.6 reshape.15.slots
  2.0 163.8 %spread.1 = (bf16[8,3,2,256,256]{4,3,2,1,0:T(8,128)(2,1)}, bf16[8,1536,512]{2,1,0:T(8,128)(2,1)}, bf16[4,1536,512]{2,1,0:T(8,128)(2,1)}) custom-call(s32[24]{0:T(128)} %reshape.15.slots, bf16[2,12,64,256]{3,2,1,0:T(8,128)(2,1)} %screen.1, bf16[1536,512]{1,0:T(8,128)(2,1)} %coeffs.1), custom_call_target="tpu_custom_call" | custom-call | tf_op jit(solution)/shard_map/spread/pallas_call | solution.py:225
  165.8 0.0 copy-start
  165.8 0.6 copy-done
  166.5 0.0 copy-start.1
  166.5 0.7 copy-done.1
  167.2 0.0 copy-start.2
  167.2 0.7 copy-done.2
  167.8 6.1 %row_sums.1 = bf16[6,256,1024]{2,1,0:T(8,128)(2,1)S(1)} custom-call(s32[1]{0:T(128)S(6)} %copy.11.count, s32[24]{0:T(128)S(1)} %bitcast.7, s32[24]{0:T(128)S(1)} %bitcast.8, s32[24]{0:T(128)S(1)} %bitcast.9, bf16[2,24,256,256]{3,2,1,0:T(8,128)(2,1)} %refs_3_.1, bf16[2,24,256,256]{3,2,1,0:T(8,128)(2,1)} %refs_3_.1, bf16[2,24,256,256]{3,2,1,0:T(8,128)(2,1)} %refs_3_.1, ...), custom_call_target="tpu_custom_call" | custom-call | tf_op jit(solution)/shard_map/row_sums/pallas_call | solution.py:296
  173.9 36.3 %scatter.1 = f32[256,1024]{1,0:T(8,128)S(1)} custom-call(bf16[4,1536,512]{2,1,0:T(8,128)(2,1)} %get-tuple-element.8.points, bf16[1536,1024]{1,0:T(8,128)(2,1)S(1)} %bitcast.6), custom_call_target="tpu_custom_call" | custom-call | tf_op jit(solution)/shard_map/scatter/pallas_call | solution.py:373
  210.2 1.9 reshape.19
Async XLA Ops:
  165.8 0.7 copy-start
  166.5 0.7 copy-start.1
  167.2 0.7 copy-start.2
